TPU v7x, 32 devices: a whole 2x2x4 slice. The times are simulated.
32 devices in a mesh: tm: 8 (over z, y), scan: 4 (over x, core).
Axes of the slice: x: 2, y: 2, z: 4, core: 2. Of those that a mesh axis runs over, the one named last changes fastest.
Arguments:
- spec_grad: float32 [1, 2, 1048576], P(None, None, 'tm'), may hold values from -6 to 6
- transients: bfloat16 [1, 32, 1048576], P(None, 'scan', 'tm')
- kernels: float32 [16, 16], replicated, may hold values from -1.5 to 1.5
- shifts: int32 [1, 32], P(None, 'scan'), may hold values from -512 to 512, as said below
- tiles: int32 [1, 32], P(None, 'scan'), may hold values from 0 to 15
Outputs:
- scan_grad: float32 [1, 32, 1048576], P(None, 'scan', 'tm')
- kernel_grad: float32 [16, 16], replicated
Inputs may be any that keep to these rules, and one draw needn't show every extreme that they name: `shifts`: in every window one scan has shift 512 and another has shift -512.
All inputs are finite; a program needn't handle non-finite values.
Results may differ from a plain program's by a relative error of at most 0.0003.
Values sent between devices are 32-bit elements; how exact they have to be, the bound alone decides.
A program may use at most 64 MiB of HBM per device.

v0:
```python
import functools
import math

import jax
import jax.numpy as jnp
import numpy as np
from jax import lax
from jax.experimental import pallas as pl
from jax.experimental.pallas import tpu as pltpu
from jax.sharding import PartitionSpec as P

N1 = 1024
N2 = 1024
TILES = 16
TAPS = 16
KMAX = 512


highest = lax.Precision.HIGHEST
high = lax.Precision.HIGH
LANES = 128
EDGE = 8
MESH = pl.DeviceIdType.MESH


def halves(x):
    top = x.astype(jnp.bfloat16)
    return top, (x - top.astype(jnp.float32)).astype(jnp.bfloat16)


def fir_kernel(chunk, shifts_ref, tiles_ref, kernels_ref, g_ref, x_ref, out_ref, table_ref,
               gg, t_hi, t_lo, corr, xs, ys):
    step = pl.program_id(0)
    scans = x_ref.shape[0]
    rows = g_ref.shape[0] - 8

    def place(s):
        start = EDGE * LANES - TAPS // 2 + 1 - shifts_ref[s]
        return start // LANES, (start // (LANES // 2)) % 2, start % (LANES // 2)

    @pl.when(step == 0)
    def _():
        gg[0] = g_ref[:rows]
        lane = lax.broadcasted_iota(jnp.int32, (rows, LANES), 1)
        here = pltpu.roll(g_ref[:rows], LANES // 2, 1)
        nxt = pltpu.roll(g_ref[1 : rows + 1], LANES // 2, 1)
        gg[1] = jnp.where(lane < LANES // 2, here, nxt)
        row = lax.broadcasted_iota(jnp.int32, (2 * LANES, LANES), 0)
        col = lax.broadcasted_iota(jnp.int32, (2 * LANES, LANES), 1)

        def band(s, carry):
            _, _, o = place(s)
            tap = o + col + (TAPS - 1) - row
            value = jnp.zeros((2 * LANES, LANES), jnp.float32)
            for j in range(TAPS):
                value = jnp.where(tap == j, kernels_ref[tiles_ref[s], j], value)
            top, rest = halves(value)
            t_hi[s] = top
            t_lo[s] = rest
            corr[s] = jnp.zeros((LANES, 2 * LANES), jnp.float32)
            return carry

        lax.fori_loop(0, scans, band, 0)

    def split_in(r, carry):
        at = pl.ds(pl.multiple_of(r * LANES, LANES), LANES)
        xs[pl.ds(pl.multiple_of(r * scans, scans), scans), :] = x_ref[:, at].astype(jnp.float32)
        return carry

    lax.fori_loop(0, chunk, split_in, 0, unroll=8)

    for s in range(scans):
        q, c, _ = place(s)
        first = step * chunk + q
        window = jnp.concatenate(
            [gg[c, pl.ds(first, chunk), :], gg[c, pl.ds(first + 1, chunk), :]], axis=1
        )
        top, rest = halves(window)
        dot = functools.partial(jnp.dot, preferred_element_type=jnp.float32)
        ys[s * chunk : (s + 1) * chunk, :] = (
            dot(top, t_hi[s]) + (dot(top, t_lo[s]) + dot(rest, t_hi[s]))
        )
        x = xs[pl.ds(s, chunk, stride=scans), :].astype(jnp.bfloat16)
        down = functools.partial(
            lax.dot_general,
            dimension_numbers=(((0,), (0,)), ((), ())),
            preferred_element_type=jnp.float32,
        )
        corr[s] += down(x, top) + down(x, rest)

    def join_out(r, carry):
        at = pl.ds(pl.multiple_of(r * LANES, LANES), LANES)
        out_ref[:, at] = ys[pl.ds(r, scans, stride=chunk), :]
        return carry

    lax.fori_loop(0, chunk, join_out, 0, unroll=8)

    @pl.when(step == pl.num_programs(0) - 1)
    def _():
        apart = lax.broadcasted_iota(jnp.int32, (LANES, 2 * LANES), 1) - lax.broadcasted_iota(
            jnp.int32, (LANES, 2 * LANES), 0
        )
        tap = lax.broadcasted_iota(jnp.int32, (TAPS, LANES), 0)
        tile = lax.broadcasted_iota(jnp.int32, (TAPS, LANES), 1)

        def fold(s, total):
            _, _, o = place(s)
            values = corr[s]
            sums = [
                jnp.sum(jnp.where(apart == o + (TAPS - 1 - j), values, 0.0), axis=0, keepdims=True)
                for j in range(TAPS)
            ]
            column = jnp.sum(jnp.concatenate(sums, axis=0), axis=1, keepdims=True)
            return total + jnp.where(tile == tiles_ref[s], column, 0.0)

        table_ref[...] = lax.fori_loop(0, scans, fold, jnp.zeros((TAPS, LANES), jnp.float32))


def scans_and_table(padded_g, x, kernels, shifts, tiles):
    scans, stretch = x.shape
    rows = stretch // LANES
    chunk = min(256, rows)
    deep = padded_g.shape[0]
    smem = pl.BlockSpec(memory_space=pltpu.SMEM)
    return pl.pallas_call(
        functools.partial(fir_kernel, chunk),
        grid=(rows // chunk,),
        out_shape=[
            jax.ShapeDtypeStruct((scans, stretch), jnp.float32),
            jax.ShapeDtypeStruct((TAPS, LANES), jnp.float32),
        ],
        in_specs=[
            smem,
            smem,
            smem,
            pl.BlockSpec((deep, LANES), lambda i: (0, 0)),
            pl.BlockSpec((scans, chunk * LANES), lambda i: (0, i)),
        ],
        out_specs=[
            pl.BlockSpec((scans, chunk * LANES), lambda i: (0, i)),
            pl.BlockSpec((TAPS, LANES), lambda i: (0, 0)),
        ],
        scratch_shapes=[
            pltpu.VMEM((2, deep - 8, LANES), jnp.float32),
            pltpu.VMEM((scans, 2 * LANES, LANES), jnp.bfloat16),
            pltpu.VMEM((scans, 2 * LANES, LANES), jnp.bfloat16),
            pltpu.VMEM((scans, LANES, 2 * LANES), jnp.float32),
            pltpu.VMEM((scans * chunk, LANES), jnp.float32),
            pltpu.VMEM((scans * chunk, LANES), jnp.float32),
        ],
        compiler_params=pltpu.CompilerParams(vmem_limit_bytes=40 * 2**20),
        name="fir",
    )(shifts, tiles, kernels, padded_g, x)


def sum_kernel(sizes, in_ref, out_ref, first, second, send, recv, send2, recv2):
    here = [lax.axis_index("tm"), lax.axis_index("scan")]
    barrier = pltpu.get_barrier_semaphore()

    def peer(axis, k):
        other = list(here)
        other[axis] = lax.rem(here[axis] + k, sizes[axis])
        return tuple(other)

    for axis in range(2):
        for k in range(1, sizes[axis]):
            pl.semaphore_signal(barrier, inc=1, device_id=peer(axis, k), device_id_type=MESH)
    pl.semaphore_wait(barrier, sizes[0] + sizes[1] - 2)
    value = in_ref[...]
    for axis, slots, out_sem, in_sem in ((0, first, send, recv), (1, second, send2, recv2)):
        slots[here[axis]] = value
        copies = [
            pltpu.make_async_remote_copy(
                src_ref=slots.at[here[axis]],
                dst_ref=slots.at[here[axis]],
                send_sem=out_sem.at[k],
                recv_sem=in_sem.at[k],
                device_id=peer(axis, k),
                device_id_type=MESH,
            )
            for k in range(1, sizes[axis])
        ]
        for copy in copies:
            copy.start()
        for copy in copies:
            copy.wait()
        value = slots[0]
        for k in range(1, sizes[axis]):
            value = value + slots[k]
    out_ref[...] = value


def sum_everywhere(table, sizes):
    dma = pltpu.SemaphoreType.DMA
    vmem = pl.BlockSpec(memory_space=pltpu.VMEM)
    return pl.pallas_call(
        functools.partial(sum_kernel, sizes),
        out_shape=jax.ShapeDtypeStruct(table.shape, table.dtype),
        in_specs=[vmem],
        out_specs=vmem,
        scratch_shapes=[
            pltpu.VMEM((sizes[0],) + table.shape, table.dtype),
            pltpu.VMEM((sizes[1],) + table.shape, table.dtype),
            dma((sizes[0],)),
            dma((sizes[0],)),
            dma((sizes[1],)),
            dma((sizes[1],)),
        ],
        compiler_params=pltpu.CompilerParams(collective_id=1, has_side_effects=True),
        name="table_sum",
    )(table)


def padded(cells, sides, width):
    for axis, dim in sides:
        count = lax.axis_size(axis)
        ends = count - 1
        head = lax.slice_in_dim(cells, 0, width, axis=dim)
        tail = lax.slice_in_dim(cells, cells.shape[dim] - width, cells.shape[dim], axis=dim)
        cells = jnp.concatenate(
            [
                lax.ppermute(tail, axis, [(i, (i + 1) % count) for i in range(ends)]),
                cells,
                lax.ppermute(head, axis, [((i + 1) % count, i) for i in range(ends)]),
            ],
            axis=dim,
        )
    return cells


def angles(left, right, period):
    product = left[:, None] * right[None, :] % period
    return 2.0 * math.pi / period * product.astype(jnp.float32)


def two_terms(table):
    table = np.asarray(table, np.float32)
    top = table.astype(jnp.bfloat16)
    return top, (table - top.astype(np.float32)).astype(jnp.bfloat16)


@functools.lru_cache
def transform_tables(n_tm, n_scan):
    devices = n_tm * n_scan
    pairs = N1 // 2 // devices
    index = np.arange(N2)
    angle = 2.0 * np.pi / N2 * (index[:, None] * index[None, :] % N2)
    slots = np.arange(N1 // 2).reshape(devices, pairs)
    mirror = np.where(slots == 0, N1 // 2, N1 - slots)
    residues = np.concatenate([slots, mirror], axis=1)
    turn = 2.0 * np.pi / (N1 * N2) * (residues[:, :, None] * index)
    time = np.arange(N1).reshape(n_tm, n_scan, -1).transpose(1, 0, 2).reshape(-1)
    last = 2.0 * np.pi / N1 * (time[:, None, None] * slots[None] % N1)
    minus = np.where(slots[None] == 0, 1.0 - 2.0 * (time[:, None, None] % 2), -np.sin(last))
    final = np.concatenate([np.cos(last), minus], axis=2).reshape(n_scan, N1 // n_scan, N1)
    final = final * float(N1 * N2) ** -0.5
    return (
        *two_terms(np.cos(angle)),
        *two_terms(np.sin(angle)),
        np.cos(turn).astype(np.float32),
        np.sin(turn).astype(np.float32),
        *two_terms(final),
    )


def transform_kernel(n_tm, n_scan, spec_ref, cos_h, cos_l, sin_h, sin_l, turn_c, turn_s, fin_h, fin_l, out_ref,
                     vcos_h, vcos_l, vsin_h, vsin_l, vturn_c, vturn_s, vfin_h, vfin_l,
                     x_out, x_in, b_out, b_all, y_out, y_all, e_out, e_in, local_sem, send, recv):
    d, s = lax.axis_index("tm"), lax.axis_index("scan")
    mine = s * n_tm + d
    pairs = x_out.shape[1] // 2
    barrier = pltpu.get_barrier_semaphore()
    lines = [(lax.rem(d + k, n_tm), s) for k in range(1, n_tm)]
    columns = [(d, lax.rem(s + k, n_scan)) for k in range(1, n_scan)]
    for peer in lines + columns:
        pl.semaphore_signal(barrier, inc=1, device_id=peer, device_id_type=MESH)

    loads = [
        pltpu.make_async_copy(source, target, local_sem.at[i])
        for i, (source, target) in enumerate(
            (
                (cos_h, vcos_h),
                (cos_l, vcos_l),
                (sin_h, vsin_h),
                (sin_l, vsin_l),
                (turn_c.at[mine], vturn_c),
                (turn_s.at[mine], vturn_s),
                (fin_h.at[s], vfin_h),
                (fin_l.at[s], vfin_l),
            )
        )
    ]
    for load in loads:
        load.start()

    def remote(phase, k, source, target, peer):
        return pltpu.make_async_remote_copy(
            src_ref=source,
            dst_ref=target,
            send_sem=send.at[phase, k],
            recv_sem=recv.at[phase, k],
            device_id=peer,
            device_id_type=MESH,
        )

    def exchange(phase, blocks, target):
        copies = [
            remote(phase, k, blocks.at[peer[0]], target, peer) for k, peer in enumerate(lines)
        ]
        for copy in copies:
            copy.start()
        return copies

    def spread(phase, block):
        copies = [remote(phase, k, block, block, peer) for k, peer in enumerate(columns)]
        for copy in copies:
            copy.start()
        return copies

    def finish(copies):
        for copy in copies:
            copy.wait()

    dot = functools.partial(jnp.dot, preferred_element_type=jnp.float32)
    across = functools.partial(
        lax.dot_general,
        dimension_numbers=(((1,), (1,)), ((), ())),
        preferred_element_type=jnp.float32,
    )
    height = n_tm * 2 * pairs
    row = lax.broadcasted_iota(jnp.int32, (height, N1), 0)
    col = lax.broadcasted_iota(jnp.int32, (height, N1), 1)
    inner = row % (2 * pairs)
    slot = pairs * (s * n_tm + row // (2 * pairs)) + inner % pairs
    partner = jnp.where(slot == 0, N1 // 2, N1 - slot)
    pick = jnp.where(col == jnp.where(inner < pairs, slot, partner), 1.0, 0.0).astype(jnp.bfloat16)
    top, rest = halves(spec_ref[...])
    x_out[...] = (across(pick, top) + across(pick, rest)).reshape(x_out.shape)
    pl.semaphore_wait(barrier, len(lines) + len(columns))
    moving = exchange(0, x_out, x_in.at[d])
    x_in[d] = x_out[d]
    for load in loads:
        load.wait()
    finish(moving)

    real = jnp.concatenate([x_in[i, :, :LANES] for i in range(n_tm)], axis=1)
    imag = jnp.concatenate([x_in[i, :, LANES:] for i in range(n_tm)], axis=1)
    top, rest = halves(jnp.concatenate([real, imag], axis=0))
    both = jnp.concatenate([top, rest], axis=0)
    count = 4 * pairs

    def turned(high_table, low_table):
        big = dot(both, high_table[...])
        total = big[:count] + (big[count:] + dot(top, low_table[...]))
        return total[: 2 * pairs], total[2 * pairs :]

    re_cos, im_cos = turned(vcos_h, vcos_l)
    re_sin, im_sin = turned(vsin_h, vsin_l)
    part_re = re_cos - im_sin
    part_im = re_sin + im_cos
    a_re = vturn_c[...] * part_re - vturn_s[...] * part_im
    a_im = vturn_s[...] * part_re + vturn_c[...] * part_im
    alone = jnp.logical_and(lax.broadcasted_iota(jnp.int32, (pairs, N2), 0) == 0, mine == 0)
    b_re = jnp.where(alone, a_re[:pairs], a_re[:pairs] + a_re[pairs:])
    b_im = jnp.where(alone, a_re[pairs:], a_im[:pairs] - a_im[pairs:])
    for i in range(n_tm):
        b_out[i, :pairs] = b_re[:, i * LANES : (i + 1) * LANES]
        b_out[i, pairs:] = b_im[:, i * LANES : (i + 1) * LANES]
    moving = exchange(1, b_out, b_all.at[s, d])
    b_all[s, d] = b_out[d]
    finish(moving)
    finish(spread(2, b_all.at[s]))

    top, rest = halves(b_all[...].reshape(N1, LANES))
    rows_out = dot(vfin_h[...], top) + (dot(vfin_h[...], rest) + dot(vfin_l[...], top))
    y_out[...] = rows_out.reshape(y_out.shape)
    moving = exchange(3, y_out, y_all.at[s, d])
    y_all[s, d] = y_out[d]
    finish(moving)
    finish(spread(4, y_all.at[s]))

    deep = y_out.shape[1]
    for i in range(n_scan):
        for j in range(n_tm):
            out_ref[pl.ds(EDGE + i * deep * n_tm + j, deep, stride=n_tm), :] = y_all[i, j]
    stretch = n_scan * n_tm * deep
    e_out[0] = out_ref[EDGE : 2 * EDGE]
    e_out[1] = out_ref[stretch : stretch + EDGE]
    edges = [
        remote(5, 0, e_out.at[1], e_in.at[0], (lax.rem(d + 1, n_tm), s)),
        remote(5, 1, e_out.at[0], e_in.at[1], (lax.rem(d + n_tm - 1, n_tm), s)),
    ]
    for copy in edges:
        copy.start()
    finish(edges)
    out_ref[:EDGE] = jnp.where(d == 0, 0.0, e_in[0])
    out_ref[EDGE + stretch : 2 * EDGE + stretch] = jnp.where(d == n_tm - 1, 0.0, e_in[1])
    out_ref[2 * EDGE + stretch :] = jnp.zeros((8, LANES), jnp.float32)


def transform(spec, n_tm, n_scan):
    tables = [jnp.asarray(t) for t in transform_tables(n_tm, n_scan)]
    pairs = N1 // 2 // (n_tm * n_scan)
    part = N1 // n_tm // n_scan
    rows = N1 // n_tm * N2 // LANES
    dma = pltpu.SemaphoreType.DMA
    f32, bf16 = jnp.float32, jnp.bfloat16
    vmem = pl.BlockSpec(memory_space=pltpu.VMEM)
    return pl.pallas_call(
        functools.partial(transform_kernel, n_tm, n_scan),
        out_shape=jax.ShapeDtypeStruct((rows + 2 * EDGE + 8, LANES), f32),
        in_specs=[vmem] + [pl.BlockSpec(memory_space=pl.ANY)] * len(tables),
        out_specs=vmem,
        scratch_shapes=[
            pltpu.VMEM((N2, N2), bf16),
            pltpu.VMEM((N2, N2), bf16),
            pltpu.VMEM((N2, N2), bf16),
            pltpu.VMEM((N2, N2), bf16),
            pltpu.VMEM((2 * pairs, N2), f32),
            pltpu.VMEM((2 * pairs, N2), f32),
            pltpu.VMEM((N1 // n_scan, N1), bf16),
            pltpu.VMEM((N1 // n_scan, N1), bf16),
            pltpu.VMEM((n_tm, 2 * pairs, 2 * LANES), f32),
            pltpu.VMEM((n_tm, 2 * pairs, 2 * LANES), f32),
            pltpu.VMEM((n_tm, 2 * pairs, LANES), f32),
            pltpu.VMEM((n_scan, n_tm, 2 * pairs, LANES), f32),
            pltpu.VMEM((n_tm, part, LANES), f32),
            pltpu.VMEM((n_scan, n_tm, part, LANES), f32),
            pltpu.VMEM((2, EDGE, LANES), f32),
            pltpu.VMEM((2, EDGE, LANES), f32),
            dma((len(tables),)),
            dma((6, n_tm)),
            dma((6, n_tm)),
        ],
        compiler_params=pltpu.CompilerParams(
            collective_id=2, has_side_effects=True, vmem_limit_bytes=40 * 2**20
        ),
        name="transform",
    )(spec, *tables)


def general_transform(spec_grad):
    n_tm = lax.axis_size("tm")
    tm_index = lax.axis_index("tm")
    windows = spec_grad.shape[0]
    stretch = spec_grad.shape[2]
    total = N1 * N2
    rows_f2 = N2 // n_tm
    rows_f1 = N1 // n_tm
    local = spec_grad.reshape(windows, 2, rows_f2, N1)
    moved = lax.all_to_all(local, "tm", split_axis=3, concat_axis=2, tiled=True)
    freq_two = jnp.arange(N2, dtype=jnp.int32)
    freq_one = tm_index * rows_f1 + jnp.arange(rows_f1, dtype=jnp.int32)
    time_two = jnp.arange(N2, dtype=jnp.int32)
    phase_two = angles(freq_two, time_two, N2)
    cos_two = jnp.cos(phase_two)
    sin_two = jnp.sin(phase_two)
    real_in = moved[:, 0]
    imag_in = moved[:, 1]
    part_re = jnp.einsum("wfa,ft->wat", real_in, cos_two, precision=high) - jnp.einsum(
        "wfa,ft->wat", imag_in, sin_two, precision=high
    )
    part_im = jnp.einsum("wfa,ft->wat", real_in, sin_two, precision=high) + jnp.einsum(
        "wfa,ft->wat", imag_in, cos_two, precision=high
    )
    twiddle = angles(freq_one, time_two, total)
    cos_tw = jnp.cos(twiddle)[None]
    sin_tw = jnp.sin(twiddle)[None]
    turned = jnp.stack(
        [part_re * cos_tw - part_im * sin_tw, part_re * sin_tw + part_im * cos_tw], 1
    )
    columns = lax.all_to_all(turned, "tm", split_axis=3, concat_axis=2, tiled=True)
    all_one = jnp.arange(N1, dtype=jnp.int32)
    phase_one = angles(all_one, all_one, N1)
    rows_out = jnp.einsum("wfb,ft->wbt", columns[:, 0], jnp.cos(phase_one), precision=high)
    rows_out = rows_out - jnp.einsum(
        "wfb,ft->wbt", columns[:, 1], jnp.sin(phase_one), precision=high
    )
    rows_out = rows_out * total ** (-0.5)
    placed = lax.all_to_all(rows_out, "tm", split_axis=2, concat_axis=1, tiled=True)
    avg_grad = jnp.transpose(placed, (0, 2, 1)).reshape(windows, stretch)
    cells = padded(avg_grad, (("tm", 1),), EDGE * LANES).reshape(windows, -1, LANES)
    return jnp.pad(cells, ((0, 0), (0, 8), (0, 0)))


def on_device(spec_grad, transients, kernels, shifts, tiles):
    n_tm, n_scan = lax.axis_size("tm"), lax.axis_size("scan")
    windows = spec_grad.shape[0]
    if windows == 1 and N2 // n_tm == LANES and N1 // 2 % (8 * n_tm * n_scan) == 0:
        cells = transform(spec_grad.reshape(2 * LANES, N1), n_tm, n_scan)[None]
    else:
        cells = general_transform(spec_grad)
    table, scan_grad = None, []
    for w in range(windows):
        rows_w, table_w = scans_and_table(cells[w], transients[w], kernels, shifts[w], tiles[w])
        scan_grad.append(rows_w)
        table = table_w if table is None else table + table_w
    scan_grad = jnp.stack(scan_grad)
    sizes = (n_tm, n_scan)
    if sizes[0] <= 8:
        table = sum_everywhere(table, sizes)
    else:
        table = lax.psum(table, ("tm", "scan"))
    return (scan_grad, table[:, :TILES].T)


def solution(mesh):
    placed = (P(None, None, "tm"), P(None, "scan", "tm"), P(), P(None, "scan"), P(None, "scan"))
    return jax.shard_map(
        on_device,
        mesh=mesh,
        in_specs=placed,
        out_specs=(P(None, "scan", "tm"), P()),
        check_vma=False,
    )
```

profile of v0, /device:TPU:0, one launch (start us, length us, event | category | flops | bytes accessed | tf_op | source)
XLA Modules:
  0.0 82.2 jit_solution(7799714065617056410)
XLA Ops:
  0.6 0.0 copy-start
  0.6 2.3 %reshape.7.spec_ref = f32[256,1024]{1,0:T(8,128)S(1)} reshape(f32[1,2,131072]{2,1,0:T(2,128)} %param.13) | data formatting | bytes 2097152 | tf_op jit(solution)/shard_map/reshape | solution.py:490
  2.9 0.0 copy-done
  2.9 0.0 copy-start.1
  2.9 1.6 %copy-done.1 = bf16[4,256,1024]{2,1,0:T(8,128)(2,1)S(1)} copy-done((bf16[4,256,1024]{2,1,0:T(8,128)(2,1)S(1)}, bf16[4,256,1024]{2,1,0:T(8,128)(2,1)}, u32[]{:S(2)}) %copy-start.1) | copy-done | bytes 2097176
  4.5 0.0 copy-start.2
  4.5 1.6 %copy-done.2 = bf16[1024,1024]{1,0:T(8,128)(2,1)S(1)} copy-done((bf16[1024,1024]{1,0:T(8,128)(2,1)S(1)}, bf16[1024,1024]{1,0:T(8,128)(2,1)}, u32[]{:S(2)}) %copy-start.2) | copy-done | bytes 2097176
  6.1 0.0 copy-start.3
  6.1 1.6 %copy-done.3 = bf16[1024,1024]{1,0:T(8,128)(2,1)S(1)} copy-done((bf16[1024,1024]{1,0:T(8,128)(2,1)S(1)}, bf16[1024,1024]{1,0:T(8,128)(2,1)}, u32[]{:S(2)}) %copy-start.3) | copy-done | bytes 2097176
  7.7 0.0 copy-start.4
  7.7 1.6 %copy-done.4 = bf16[1024,1024]{1,0:T(8,128)(2,1)S(1)} copy-done((bf16[1024,1024]{1,0:T(8,128)(2,1)S(1)}, bf16[1024,1024]{1,0:T(8,128)(2,1)}, u32[]{:S(2)}) %copy-start.4) | copy-done | bytes 2097176
  9.3 0.0 copy-start.5
  9.3 1.6 %copy-done.5 = bf16[1024,1024]{1,0:T(8,128)(2,1)S(1)} copy-done((bf16[1024,1024]{1,0:T(8,128)(2,1)S(1)}, bf16[1024,1024]{1,0:T(8,128)(2,1)}, u32[]{:S(2)}) %copy-start.5) | copy-done | bytes 2097176
  10.9 0.0 copy-start.6
  10.9 0.0 copy-start.7
  10.9 0.0 copy-start.9
  10.9 0.0 copy-start.10
  10.9 42.0 %transform.1.g_ref = f32[1048,128]{1,0:T(8,128)S(1)} custom-call(f32[256,1024]{1,0:T(8,128)S(1)} %reshape.7.spec_ref, bf16[1024,1024]{1,0:T(8,128)(2,1)S(1)} %copy-done.5, bf16[1024,1024]{1,0:T(8,128)(2,1)S(1)} %copy-done.4, bf16[1024,1024]{1,0:T(8,128)(2,1)S(1)} %copy-done.3, bf16[1024,1024]{1,0:T(8,128)(2,1)S(1)} %copy-done.2, ...), custom_call_target="tpu_custom_call" | custom-call | tf_op jit(solution)/shard_map/transform/pallas_call | solution.py:409
  52.9 0.0 copy-done.6
  52.9 0.0 copy-done.7
  53.0 0.0 copy-done.9
  53.0 0.0 copy-done.10
  53.0 16.6 %fir.1 = (f32[8,131072]{1,0:T(8,128)}, f32[16,128]{1,0:T(8,128)S(1)}) custom-call(s32[8]{0:T(128)S(1)} %bitcast.7, s32[8]{0:T(128)S(1)} %bitcast.8, f32[16,16]{1,0:T(8,128)S(1)} %copy-done.7, f32[1048,128]{1,0:T(8,128)S(1)} %transform.1.g_ref, bf16[8,131072]{1,0:T(8,128)(2,1)S(1)} %bitcast.6), custom_call_target="tpu_custom_call" | custom-call | tf_op jit(solution)/shard_map/fir/pallas_call | solution.py:125
  69.6 0.0 copy-start.8
  69.6 0.6 copy-done.8
  70.2 10.6 %table_sum.1 = f32[16,128]{1,0:T(8,128)} custom-call(f32[16,128]{1,0:T(8,128)} %copy-done.8), custom_call_target="tpu_custom_call" | custom-call | tf_op jit(solution)/shard_map/table_sum/pallas_call | solution.py:196
  80.8 0.7 slice_bitcast_fusion
  81.5 0.7 copy.15
Async XLA Ops:
  0.6 2.3 %copy-start = (bf16[4,256,1024]{2,1,0:T(8,128)(2,1)S(1)}, bf16[4,256,1024]{2,1,0:T(8,128)(2,1)}, u32[]{:S(2)}) copy-start(bf16[4,256,1024]{2,1,0:T(8,128)(2,1)} %constant.23.clone.fin_l) | copy-start | bytes 6291460
  2.9 1.6 %copy-start.1 = (bf16[4,256,1024]{2,1,0:T(8,128)(2,1)S(1)}, bf16[4,256,1024]{2,1,0:T(8,128)(2,1)}, u32[]{:S(2)}) copy-start(bf16[4,256,1024]{2,1,0:T(8,128)(2,1)} %constant.22.clone.fin_h) | copy-start | bytes 6291460
  4.5 1.6 %copy-start.2 = (bf16[1024,1024]{1,0:T(8,128)(2,1)S(1)}, bf16[1024,1024]{1,0:T(8,128)(2,1)}, u32[]{:S(2)}) copy-start(bf16[1024,1024]{1,0:T(8,128)(2,1)} %constant.19.clone.sin_l) | copy-start | bytes 6291460
  6.1 1.6 %copy-start.3 = (bf16[1024,1024]{1,0:T(8,128)(2,1)S(1)}, bf16[1024,1024]{1,0:T(8,128)(2,1)}, u32[]{:S(2)}) copy-start(bf16[1024,1024]{1,0:T(8,128)(2,1)} %constant.18.clone.sin_h) | copy-start | bytes 6291460
  7.7 1.6 %copy-start.4 = (bf16[1024,1024]{1,0:T(8,128)(2,1)S(1)}, bf16[1024,1024]{1,0:T(8,128)(2,1)}, u32[]{:S(2)}) copy-start(bf16[1024,1024]{1,0:T(8,128)(2,1)} %constant.17.clone.cos_l) | copy-start | bytes 6291460
  9.3 1.6 %copy-start.5 = (bf16[1024,1024]{1,0:T(8,128)(2,1)S(1)}, bf16[1024,1024]{1,0:T(8,128)(2,1)}, u32[]{:S(2)}) copy-start(bf16[1024,1024]{1,0:T(8,128)(2,1)} %constant.16.clone.cos_h) | copy-start | bytes 6291460
  10.9 42.1 %copy-start.6 = (bf16[1,8,131072]{2,1,0:T(8,128)(2,1)S(1)}, bf16[1,8,131072]{2,1,0:T(8,128)(2,1)}, u32[]{:S(2)}) copy-start(bf16[1,8,131072]{2,1,0:T(8,128)(2,1)} %param.14) | copy-start | bytes 6291460
  10.9 42.1 %copy-start.7 = (f32[16,16]{1,0:T(8,128)S(1)}, f32[16,16]{1,0:T(8,128)}, u32[]{:S(2)}) copy-start(f32[16,16]{1,0:T(8,128)} %kernels_ref.1) | copy-start | bytes 3076
  10.9 42.1 %copy-start.9 = (s32[1,8]{1,0:T(1,128)S(1)}, s32[1,8]{1,0:T(1,128)}, u32[]{:S(2)}) copy-start(s32[1,8]{1,0:T(1,128)} %param.16) | copy-start | bytes 100
  10.9 42.1 %copy-start.10 = (s32[1,8]{1,0:T(1,128)S(1)}, s32[1,8]{1,0:T(1,128)}, u32[]{:S(2)}) copy-start(s32[1,8]{1,0:T(1,128)} %param.17) | copy-start | bytes 100
  69.6 0.6 copy-start.8
where the time goes:
time: 82.5 us; the launch traced here: 82.2 us
  Pallas kernels  69.3 us (84%)
  local copies, waits for them, and re-layouts  12.2 us (15%)
    pallas_call x1, Pallas kernels, transform(): pl.pallas_call(functools.partial(transform_kernel, n_tm, n_scan), out_sha...  42 us
    pallas_call x1, Pallas kernels, scans_and_table(): pl.pallas_call(functools.partial(fir_kernel, chunk), grid=(rows // chunk,...  16.6 us
    pallas_call x1, Pallas kernels, sum_everywhere(): pl.pallas_call(functools.partial(sum_kernel, sizes), out_shape=jax.ShapeD...  10.6 us
    unnamed x23, local copies, waits for them, and re-layouts  9.24 us
    reshape x1, local copies, waits for them, and re-layouts, on_device(): cells = transform(spec_grad.reshape(2 * LANES, N1), n_tm, n_scan)[None]  2.27 us

commit v1 on v0

--- a/solution.py
+++ b/solution.py
@@ -111,7 +111,8 @@
                 for j in range(TAPS)
             ]
             column = jnp.sum(jnp.concatenate(sums, axis=0), axis=1, keepdims=True)
-            return total + jnp.where(tile == tiles_ref[s], column, 0.0)
+            line = jnp.sum(jnp.where(tap == tile, column, 0.0), axis=0, keepdims=True)
+            return total + jnp.where(tap == tiles_ref[s], line, 0.0)
 
         table_ref[...] = lax.fori_loop(0, scans, fold, jnp.zeros((TAPS, LANES), jnp.float32))
 
@@ -187,7 +188,7 @@
         value = slots[0]
         for k in range(1, sizes[axis]):
             value = value + slots[k]
-    out_ref[...] = value
+    out_ref[...] = value[:, :TAPS]
 
 
 def sum_everywhere(table, sizes):
@@ -195,7 +196,7 @@
     vmem = pl.BlockSpec(memory_space=pltpu.VMEM)
     return pl.pallas_call(
         functools.partial(sum_kernel, sizes),
-        out_shape=jax.ShapeDtypeStruct(table.shape, table.dtype),
+        out_shape=jax.ShapeDtypeStruct((TILES, TAPS), table.dtype),
         in_specs=[vmem],
         out_specs=vmem,
         scratch_shapes=[
@@ -265,13 +266,14 @@
 
 def transform_kernel(n_tm, n_scan, spec_ref, cos_h, cos_l, sin_h, sin_l, turn_c, turn_s, fin_h, fin_l, out_ref,
                      vcos_h, vcos_l, vsin_h, vsin_l, vturn_c, vturn_s, vfin_h, vfin_l,
-                     x_out, x_in, b_out, b_all, y_out, y_all, e_out, e_in, local_sem, send, recv):
+                     x_out, x_in, b_out, b_all, y_out, y_all, e_out, e_in, local_sem, send, recv,
+                     pass_send, pass_recv):
     d, s = lax.axis_index("tm"), lax.axis_index("scan")
     mine = s * n_tm + d
     pairs = x_out.shape[1] // 2
     barrier = pltpu.get_barrier_semaphore()
     lines = [(lax.rem(d + k, n_tm), s) for k in range(1, n_tm)]
-    columns = [(d, lax.rem(s + k, n_scan)) for k in range(1, n_scan)]
+    columns = [(d, s + 1 - 2 * lax.rem(s, 2)), (d, lax.rem(s + 2, n_scan))]
     for peer in lines + columns:
         pl.semaphore_signal(barrier, inc=1, device_id=peer, device_id_type=MESH)
 
@@ -311,11 +313,39 @@
             copy.start()
         return copies
 
-    def spread(phase, block):
-        copies = [remote(phase, k, block, block, peer) for k, peer in enumerate(columns)]
-        for copy in copies:
+    mate, across_x = s + 1 - 2 * lax.rem(s, 2), lax.rem(s + 2, n_scan)
+
+    def share(phase, blocks, full):
+        moving = exchange(phase, blocks, full.at[s, d])
+        full[s, d] = blocks[d]
+        owners = [lax.rem(d + n_tm - k, n_tm) for k in range(n_tm)]
+
+        def step(kind, j, row, column):
+            block = full.at[row, owners[j]]
+            copy = pltpu.make_async_remote_copy(
+                src_ref=block,
+                dst_ref=block,
+                send_sem=pass_send.at[phase - 1, kind, j],
+                recv_sem=pass_recv.at[phase - 1, kind, j],
+                device_id=(d, column),
+                device_id_type=MESH,
+            )
             copy.start()
-        return copies
+            return copy
+
+        far, near, relayed = [], [], []
+        for j in range(n_tm):
+            if j:
+                moving[j - 1].wait_recv()
+            far.append(step(0, j, s, across_x))
+            near.append(step(1, j, s, mate))
+        for j in range(n_tm):
+            far[j].wait_recv()
+            relayed.append(step(2, j, across_x, mate))
+        for copy in near + relayed:
+            copy.wait_recv()
+        for copy in moving + far + near + relayed:
+            copy.wait_send()
 
     def finish(copies):
         for copy in copies:
@@ -366,18 +396,12 @@
     for i in range(n_tm):
         b_out[i, :pairs] = b_re[:, i * LANES : (i + 1) * LANES]
         b_out[i, pairs:] = b_im[:, i * LANES : (i + 1) * LANES]
-    moving = exchange(1, b_out, b_all.at[s, d])
-    b_all[s, d] = b_out[d]
-    finish(moving)
-    finish(spread(2, b_all.at[s]))
+    share(1, b_out, b_all)
 
     top, rest = halves(b_all[...].reshape(N1, LANES))
     rows_out = dot(vfin_h[...], top) + (dot(vfin_h[...], rest) + dot(vfin_l[...], top))
     y_out[...] = rows_out.reshape(y_out.shape)
-    moving = exchange(3, y_out, y_all.at[s, d])
-    y_all[s, d] = y_out[d]
-    finish(moving)
-    finish(spread(4, y_all.at[s]))
+    share(2, y_out, y_all)
 
     deep = y_out.shape[1]
     for i in range(n_scan):
@@ -387,8 +411,8 @@
     e_out[0] = out_ref[EDGE : 2 * EDGE]
     e_out[1] = out_ref[stretch : stretch + EDGE]
     edges = [
-        remote(5, 0, e_out.at[1], e_in.at[0], (lax.rem(d + 1, n_tm), s)),
-        remote(5, 1, e_out.at[0], e_in.at[1], (lax.rem(d + n_tm - 1, n_tm), s)),
+        remote(3, 0, e_out.at[1], e_in.at[0], (lax.rem(d + 1, n_tm), s)),
+        remote(3, 1, e_out.at[0], e_in.at[1], (lax.rem(d + n_tm - 1, n_tm), s)),
     ]
     for copy in edges:
         copy.start()
@@ -429,11 +453,13 @@
             pltpu.VMEM((2, EDGE, LANES), f32),
             pltpu.VMEM((2, EDGE, LANES), f32),
             dma((len(tables),)),
-            dma((6, n_tm)),
-            dma((6, n_tm)),
+            dma((4, n_tm)),
+            dma((4, n_tm)),
+            dma((2, 3, n_tm)),
+            dma((2, 3, n_tm)),
         ],
         compiler_params=pltpu.CompilerParams(
-            collective_id=2, has_side_effects=True, vmem_limit_bytes=40 * 2**20
+            collective_id=2, has_side_effects=True, vmem_limit_bytes=58 * 2**20
         ),
         name="transform",
     )(spec, *tables)
@@ -486,7 +512,7 @@
 def on_device(spec_grad, transients, kernels, shifts, tiles):
     n_tm, n_scan = lax.axis_size("tm"), lax.axis_size("scan")
     windows = spec_grad.shape[0]
-    if windows == 1 and N2 // n_tm == LANES and N1 // 2 % (8 * n_tm * n_scan) == 0:
+    if windows == 1 and n_scan == 4 and N2 // n_tm == LANES and N1 // 2 % (8 * n_tm * n_scan) == 0:
         cells = transform(spec_grad.reshape(2 * LANES, N1), n_tm, n_scan)[None]
     else:
         cells = general_transform(spec_grad)
@@ -500,8 +526,8 @@
     if sizes[0] <= 8:
         table = sum_everywhere(table, sizes)
     else:
-        table = lax.psum(table, ("tm", "scan"))
-    return (scan_grad, table[:, :TILES].T)
+        table = lax.psum(table[:, :TAPS], ("tm", "scan"))
+    return (scan_grad, table)
 
 
 def solution(mesh):

time: 82.5 us -> 76.8 us (0.931)
  local copies, waits for them, and re-layouts: 12.2 us -> 6.04 us
    unnamed x23 -> x13, local copies, waits for them, and re-layouts: 9.24 us -> 2.95 us
where the time goes in v1:
time: 76.8 us; the launch traced here: 76.5 us
  Pallas kernels  69.8 us (91%)
  local copies, waits for them, and re-layouts  6.04 us (8%)
    pallas_call x1, Pallas kernels, transform(): pl.pallas_call(functools.partial(transform_kernel, n_tm, n_scan), out_sha...  42.2 us
    pallas_call x1, Pallas kernels, scans_and_table(): pl.pallas_call(functools.partial(fir_kernel, chunk), grid=(rows // chunk,...  16.6 us
    pallas_call x1, Pallas kernels, sum_everywhere(): pl.pallas_call(functools.partial(sum_kernel, sizes), out_shape=jax.ShapeD...  11 us
    reshape x1, local copies, waits for them, and re-layouts, on_device(): cells = transform(spec_grad.reshape(2 * LANES, N1), n_tm, n_scan)[None]  3.09 us
    unnamed x13, local copies, waits for them, and re-layouts  2.95 us

profile of v1, /device:TPU:0, one launch (start us, length us, event | category | flops | bytes accessed | tf_op | source)
XLA Modules:
  0.0 76.5 jit_solution(18039534357222649088)
XLA Ops:
  0.6 3.1 %reshape.7.spec_ref = f32[256,1024]{1,0:T(8,128)} reshape(f32[1,2,131072]{2,1,0:T(2,128)} %param.13) | data formatting | bytes 2097152 | tf_op jit(solution)/shard_map/reshape | solution.py:516
  3.7 0.0 copy-start.1
  3.7 0.0 copy-start.2
  3.7 0.0 copy-start.4
  3.7 0.0 copy-start.5
  3.7 42.2 %transform.1.g_ref = f32[1048,128]{1,0:T(8,128)} custom-call(f32[256,1024]{1,0:T(8,128)} %reshape.7.spec_ref, bf16[1024,1024]{1,0:T(8,128)(2,1)} %constant.16.clone.cos_h, bf16[1024,1024]{1,0:T(8,128)(2,1)} %constant.17.clone.cos_l, bf16[1024,1024]{1,0:T(8,128)(2,1)} %constant.18.clone.sin_h, bf16[1024,1024]{1,0:T(8,128)(2,1)} %constant.19.clone.sin_l, ...), custom_call_target="tpu_custom_call" | custom-call | tf_op jit(solution)/shard_map/transform/pallas_call | solution.py:433
  45.9 0.0 copy-done.1
  45.9 0.0 copy-done.2
  46.0 0.0 copy-done.4
  46.0 0.0 copy-done.5
  46.0 0.0 copy-start
  46.0 1.0 %copy-done = f32[1048,128]{1,0:T(8,128)S(1)} copy-done((f32[1048,128]{1,0:T(8,128)S(1)}, f32[1048,128]{1,0:T(8,128)}, u32[]{:S(2)}) %copy-start) | copy-done | bytes 536600
  47.0 16.6 %fir.1 = (f32[8,131072]{1,0:T(8,128)}, f32[16,128]{1,0:T(8,128)S(1)}) custom-call(s32[8]{0:T(128)S(1)} %bitcast.5, s32[8]{0:T(128)S(1)} %bitcast.6, f32[16,16]{1,0:T(8,128)S(1)} %copy-done.2, f32[1048,128]{1,0:T(8,128)S(1)} %copy-done, bf16[8,131072]{1,0:T(8,128)(2,1)S(1)} %bitcast.4), custom_call_target="tpu_custom_call" | custom-call | tf_op jit(solution)/shard_map/fir/pallas_call | solution.py:126
  63.6 0.0 copy-start.3
  63.6 0.6 copy-done.3
  64.2 11.0 %table_sum.1 = f32[16,16]{1,0:T(8,128)} custom-call(f32[16,128]{1,0:T(8,128)} %copy-done.3), custom_call_target="tpu_custom_call" | custom-call | tf_op jit(solution)/shard_map/table_sum/pallas_call | solution.py:197
  75.2 1.3 %copy.16 = f32[16,16]{1,0:T(8,128)} copy(f32[16,16]{1,0:T(8,128)} %table_sum.1) | data formatting | bytes 2048
Async XLA Ops:
  3.7 42.2 %copy-start.1 = (bf16[1,8,131072]{2,1,0:T(8,128)(2,1)S(1)}, bf16[1,8,131072]{2,1,0:T(8,128)(2,1)}, u32[]{:S(2)}) copy-start(bf16[1,8,131072]{2,1,0:T(8,128)(2,1)} %param.14) | copy-start | bytes 6291460
  3.7 42.2 %copy-start.2 = (f32[16,16]{1,0:T(8,128)S(1)}, f32[16,16]{1,0:T(8,128)}, u32[]{:S(2)}) copy-start(f32[16,16]{1,0:T(8,128)} %kernels_ref.1) | copy-start | bytes 3076
  3.7 42.2 %copy-start.4 = (s32[1,8]{1,0:T(1,128)S(1)}, s32[1,8]{1,0:T(1,128)}, u32[]{:S(2)}) copy-start(s32[1,8]{1,0:T(1,128)} %param.16) | copy-start | bytes 100
  3.7 42.2 %copy-start.5 = (s32[1,8]{1,0:T(1,128)S(1)}, s32[1,8]{1,0:T(1,128)}, u32[]{:S(2)}) copy-start(s32[1,8]{1,0:T(1,128)} %param.17) | copy-start | bytes 100
  46.0 1.0 %copy-start = (f32[1048,128]{1,0:T(8,128)S(1)}, f32[1048,128]{1,0:T(8,128)}, u32[]{:S(2)}) copy-start(f32[1048,128]{1,0:T(8,128)} %transform.1.g_ref) | copy-start | bytes 1609732
  63.6 0.6 copy-start.3

commit v2 on v1

--- a/solution.py
+++ b/solution.py
@@ -67,7 +67,7 @@
         xs[pl.ds(pl.multiple_of(r * scans, scans), scans), :] = x_ref[:, at].astype(jnp.float32)
         return carry
 
-    lax.fori_loop(0, chunk, split_in, 0, unroll=8)
+    lax.fori_loop(0, chunk, split_in, 0, unroll=32)
 
     for s in range(scans):
         q, c, _ = place(s)
@@ -93,7 +93,7 @@
         out_ref[:, at] = ys[pl.ds(r, scans, stride=chunk), :]
         return carry
 
-    lax.fori_loop(0, chunk, join_out, 0, unroll=8)
+    lax.fori_loop(0, chunk, join_out, 0, unroll=32)
 
     @pl.when(step == pl.num_programs(0) - 1)
     def _():
@@ -154,40 +154,33 @@
     )(shifts, tiles, kernels, padded_g, x)
 
 
-def sum_kernel(sizes, in_ref, out_ref, first, second, send, recv, send2, recv2):
-    here = [lax.axis_index("tm"), lax.axis_index("scan")]
+def sum_kernel(sizes, in_ref, out_ref, slots, send, recv):
+    d, s = lax.axis_index("tm"), lax.axis_index("scan")
     barrier = pltpu.get_barrier_semaphore()
-
-    def peer(axis, k):
-        other = list(here)
-        other[axis] = lax.rem(here[axis] + k, sizes[axis])
-        return tuple(other)
-
-    for axis in range(2):
-        for k in range(1, sizes[axis]):
-            pl.semaphore_signal(barrier, inc=1, device_id=peer(axis, k), device_id_type=MESH)
-    pl.semaphore_wait(barrier, sizes[0] + sizes[1] - 2)
-    value = in_ref[...]
-    for axis, slots, out_sem, in_sem in ((0, first, send, recv), (1, second, send2, recv2)):
-        slots[here[axis]] = value
-        copies = [
-            pltpu.make_async_remote_copy(
-                src_ref=slots.at[here[axis]],
-                dst_ref=slots.at[here[axis]],
-                send_sem=out_sem.at[k],
-                recv_sem=in_sem.at[k],
-                device_id=peer(axis, k),
-                device_id_type=MESH,
-            )
-            for k in range(1, sizes[axis])
-        ]
-        for copy in copies:
-            copy.start()
-        for copy in copies:
-            copy.wait()
-        value = slots[0]
-        for k in range(1, sizes[axis]):
-            value = value + slots[k]
+    steps = [(i, j) for i in range(sizes[0]) for j in range(sizes[1])]
+    peers = [(lax.rem(d + i, sizes[0]), lax.rem(s + j, sizes[1])) for i, j in steps[1:]]
+    for peer in peers:
+        pl.semaphore_signal(barrier, inc=1, device_id=peer, device_id_type=MESH)
+    slots[d, s] = in_ref[...]
+    pl.semaphore_wait(barrier, len(peers))
+    copies = [
+        pltpu.make_async_remote_copy(
+            src_ref=slots.at[d, s],
+            dst_ref=slots.at[d, s],
+            send_sem=send.at[k],
+            recv_sem=recv.at[k],
+            device_id=peer,
+            device_id_type=MESH,
+        )
+        for k, peer in enumerate(peers)
+    ]
+    for copy in copies:
+        copy.start()
+    for copy in copies:
+        copy.wait()
+    value = slots[0, 0]
+    for i, j in steps[1:]:
+        value = value + slots[i, j]
     out_ref[...] = value[:, :TAPS]
 
 
@@ -200,12 +193,9 @@
         in_specs=[vmem],
         out_specs=vmem,
         scratch_shapes=[
-            pltpu.VMEM((sizes[0],) + table.shape, table.dtype),
-            pltpu.VMEM((sizes[1],) + table.shape, table.dtype),
-            dma((sizes[0],)),
-            dma((sizes[0],)),
-            dma((sizes[1],)),
-            dma((sizes[1],)),
+            pltpu.VMEM(sizes + table.shape, table.dtype),
+            dma((sizes[0] * sizes[1],)),
+            dma((sizes[0] * sizes[1],)),
         ],
         compiler_params=pltpu.CompilerParams(collective_id=1, has_side_effects=True),
         name="table_sum",
@@ -459,7 +449,7 @@
             dma((2, 3, n_tm)),
         ],
         compiler_params=pltpu.CompilerParams(
-            collective_id=2, has_side_effects=True, vmem_limit_bytes=58 * 2**20
+            collective_id=2, has_side_effects=True, vmem_limit_bytes=56 * 2**20
         ),
         name="transform",
     )(spec, *tables)

time: 76.8 us -> 75.5 us (0.983); the launches traced: 76.5 us -> 74.2 us
  Pallas kernels: 69.8 us -> 67.4 us
    pallas_call x1, Pallas kernels: 11 us -> 9.78 us  [sum_everywhere(): pl.pallas_call(functools.partial(sum_kernel, sizes), out_shape=jax.ShapeD...]
    pallas_call x1, Pallas kernels: 16.6 us -> 15.5 us  [scans_and_table(): pl.pallas_call(functools.partial(fir_kernel, chunk), grid=(rows // chunk,...]
where the time goes in v2:
time: 75.5 us; the launch traced here: 74.2 us
  Pallas kernels  67.4 us (89%)
  local copies, waits for them, and re-layouts  6.04 us (8%)
    pallas_call x1, Pallas kernels, transform(): pl.pallas_call(functools.partial(transform_kernel, n_tm, n_scan), out_sha...  42.2 us
    pallas_call x1, Pallas kernels, scans_and_table(): pl.pallas_call(functools.partial(fir_kernel, chunk), grid=(rows // chunk,...  15.5 us
    pallas_call x1, Pallas kernels, sum_everywhere(): pl.pallas_call(functools.partial(sum_kernel, sizes), out_shape=jax.ShapeD...  9.78 us
    reshape x1, local copies, waits for them, and re-layouts, on_device(): cells = transform(spec_grad.reshape(2 * LANES, N1), n_tm, n_scan)[None]  3.09 us
    unnamed x13, local copies, waits for them, and re-layouts  2.95 us

profile of v2, /device:TPU:0, one launch (start us, length us, event | category | flops | bytes accessed | tf_op | source)
XLA Modules:
  0.0 74.2 jit_solution(3149280755532733126)
XLA Ops:
  0.6 3.1 %reshape.7.spec_ref = f32[256,1024]{1,0:T(8,128)} reshape(f32[1,2,131072]{2,1,0:T(2,128)} %param.13) | data formatting | bytes 2097152 | tf_op jit(solution)/shard_map/reshape | solution.py:506
  3.7 0.0 copy-start.1
  3.7 0.0 copy-start.2
  3.7 0.0 copy-start.4
  3.7 0.0 copy-start.5
  3.7 42.2 %transform.1.g_ref = f32[1048,128]{1,0:T(8,128)} custom-call(f32[256,1024]{1,0:T(8,128)} %reshape.7.spec_ref, bf16[1024,1024]{1,0:T(8,128)(2,1)} %constant.16.clone.cos_h, bf16[1024,1024]{1,0:T(8,128)(2,1)} %constant.17.clone.cos_l, bf16[1024,1024]{1,0:T(8,128)(2,1)} %constant.18.clone.sin_h, bf16[1024,1024]{1,0:T(8,128)(2,1)} %constant.19.clone.sin_l, ...), custom_call_target="tpu_custom_call" | custom-call | tf_op jit(solution)/shard_map/transform/pallas_call | solution.py:423
  45.9 0.0 copy-done.1
  45.9 0.0 copy-done.2
  46.0 0.0 copy-done.4
  46.0 0.0 copy-done.5
  46.0 0.0 copy-start
  46.0 1.0 %copy-done = f32[1048,128]{1,0:T(8,128)S(1)} copy-done((f32[1048,128]{1,0:T(8,128)S(1)}, f32[1048,128]{1,0:T(8,128)}, u32[]{:S(2)}) %copy-start) | copy-done | bytes 536600
  47.0 15.5 %fir.1 = (f32[8,131072]{1,0:T(8,128)}, f32[16,128]{1,0:T(8,128)S(1)}) custom-call(s32[8]{0:T(128)S(1)} %bitcast.5, s32[8]{0:T(128)S(1)} %bitcast.6, f32[16,16]{1,0:T(8,128)S(1)} %copy-done.2, f32[1048,128]{1,0:T(8,128)S(1)} %copy-done, bf16[8,131072]{1,0:T(8,128)(2,1)S(1)} %bitcast.4), custom_call_target="tpu_custom_call" | custom-call | tf_op jit(solution)/shard_map/fir/pallas_call | solution.py:126
  62.5 0.0 copy-start.3
  62.5 0.6 copy-done.3
  63.1 9.8 %table_sum.1 = f32[16,16]{1,0:T(8,128)} custom-call(f32[16,128]{1,0:T(8,128)} %copy-done.3), custom_call_target="tpu_custom_call" | custom-call | tf_op jit(solution)/shard_map/table_sum/pallas_call | solution.py:190
  72.9 1.3 %copy.16 = f32[16,16]{1,0:T(8,128)} copy(f32[16,16]{1,0:T(8,128)} %table_sum.1) | data formatting | bytes 2048
Async XLA Ops:
  3.7 42.2 %copy-start.1 = (bf16[1,8,131072]{2,1,0:T(8,128)(2,1)S(1)}, bf16[1,8,131072]{2,1,0:T(8,128)(2,1)}, u32[]{:S(2)}) copy-start(bf16[1,8,131072]{2,1,0:T(8,128)(2,1)} %param.14) | copy-start | bytes 6291460
  3.7 42.2 %copy-start.2 = (f32[16,16]{1,0:T(8,128)S(1)}, f32[16,16]{1,0:T(8,128)}, u32[]{:S(2)}) copy-start(f32[16,16]{1,0:T(8,128)} %kernels_ref.1) | copy-start | bytes 3076
  3.7 42.2 %copy-start.4 = (s32[1,8]{1,0:T(1,128)S(1)}, s32[1,8]{1,0:T(1,128)}, u32[]{:S(2)}) copy-start(s32[1,8]{1,0:T(1,128)} %param.16) | copy-start | bytes 100
  3.7 42.2 %copy-start.5 = (s32[1,8]{1,0:T(1,128)S(1)}, s32[1,8]{1,0:T(1,128)}, u32[]{:S(2)}) copy-start(s32[1,8]{1,0:T(1,128)} %param.17) | copy-start | bytes 100
  46.0 1.0 %copy-start = (f32[1048,128]{1,0:T(8,128)S(1)}, f32[1048,128]{1,0:T(8,128)}, u32[]{:S(2)}) copy-start(f32[1048,128]{1,0:T(8,128)} %transform.1.g_ref) | copy-start | bytes 1609732
  62.5 0.6 copy-start.3
